TPU v7x, 256 devices: a whole 4x4x8 slice. The times are simulated.
256 devices in a mesh: leaf: 4 (over y), row: 16 (over z, x_lo), col: 4 (over x_hi, core).
Axes of the slice: x: 4 (x_hi: 2, x_lo: 2; x = x_hi * 2 + x_lo), y: 4, z: 8, core: 2. Of those that a mesh axis runs over, the one named last changes fastest.
Arguments:
- rhs_top: float32 [8192, 64], P(('leaf', 'row')), may hold values from -6 to 6
- rhs_mid: float32 [8192, 64], P(('leaf', 'row')), may hold values from -6 to 6
- rhs_low: float32 [8192, 64], P(('leaf', 'row')), may hold values from -6 to 6
- inverse_top: float32 [8192, 8192], P(('leaf', 'row'), 'col'), as said below
- inverse_mid: float32 [8192, 4096], P(('leaf', 'row'), 'col'), as said below
- inverse_low: float32 [8192, 2048], P(('leaf', 'row'), 'col'), as said below
- tiles_mid: float32 [4, 16, 4, 4, 128, 128], P('leaf', 'row', 'col'), may hold values from -0.25 to 0.25
- places_mid: int32 [4, 16, 4, 4], P('leaf', 'row', 'col'), may hold values from 0 to 15, as said below
- tiles_low: float32 [4, 16, 4, 2, 128, 128], P('leaf', 'row', 'col'), may hold values from -0.375 to 0.375
- places_low: int32 [4, 16, 4, 2], P('leaf', 'row', 'col'), may hold values from 0 to 7, as said below
Outputs:
- solved_top: float32 [8192, 64], P(('leaf', 'row'))
- solved_mid: float32 [8192, 64], P(('leaf', 'row'))
- solved_low: float32 [8192, 64], P(('leaf', 'row'))
Inputs may be any that keep to these rules, and one draw needn't show every extreme that they name: `places_mid`: within one device the 4 positions are distinct, a quarter of the device's (16) x (1) tile slots. `places_low`: within one device the 2 positions are distinct, a quarter of the device's (8) x (1) tile slots. `inverse_top`: each separator's square block is lower triangular with positive diagonal. `inverse_mid`: each separator's square block is lower triangular with positive diagonal. `inverse_low`: each separator's square block is lower triangular with positive diagonal.
All inputs are finite; a program needn't handle non-finite values.
Results may differ from a plain program's by a relative error of at most 0.00014.
Values sent between devices are 32-bit elements; how exact they have to be, the bound alone decides.
A program may use at most 64 MiB of HBM per device.

v0:
```python
import jax
import jax.numpy as jnp
from jax import lax
from jax.sharding import PartitionSpec as P

highest = lax.Precision.HIGHEST


def partner(block, axis, apart):
    count = lax.axis_size(axis)
    route = []
    for low in range(count):
        high = low | 1 << apart
        if high != low and high < count:
            route += [(low, high), (high, low)]
    return lax.ppermute(block, axis, route)


def group_total(part, leaf_bits_used):
    col_size, vec_width = part.shape
    folded = part.reshape(col_size // 2, 2 * vec_width)
    share_part = lax.psum_scatter(folded, "row", scatter_dimension=0, tiled=True)
    for bit_index in range(leaf_bits_used):
        share_part = share_part + partner(share_part, "leaf", bit_index)
    summed = lax.all_gather(share_part, "row", axis=0, tiled=True)
    return summed.reshape(col_size, vec_width)


def col_total(part):
    return lax.psum(part, "col")


def col_pair(first_part, second_part):
    return lax.psum((first_part, second_part), "col")


def into_columns(own_vec, shift, col_size):
    own_count, vec_width = own_vec.shape
    padded = jnp.zeros((col_size + 2 * own_count, vec_width), jnp.float32)
    begin_at = jnp.clip(shift + own_count, 0, col_size + own_count)
    placed = lax.dynamic_update_slice_in_dim(padded, own_vec, begin_at, 0)
    return placed[own_count : own_count + col_size]


def from_columns(columns, shift, own_count):
    col_size = columns.shape[0]
    padded = jnp.pad(columns, ((own_count, own_count), (0, 0)))
    begin_at = jnp.clip(shift + own_count, 0, col_size + own_count)
    return lax.dynamic_slice_in_dim(padded, begin_at, own_count, 0)


def forward(inverse, columns):
    return jnp.dot(inverse, columns, precision=highest, preferred_element_type=jnp.float32)


def backward(inverse, own_vec):
    return lax.dot_general(
        inverse,
        own_vec,
        (((0,), (0,)), ((), ())),
        precision=highest,
        preferred_element_type=jnp.float32,
    )


def lift_tiles(tile_set, places, child_vec, col_size):
    tile_count = places.shape[-1]
    tile_size = tile_set.shape[-1]
    per_row = child_vec.shape[0] // tile_size
    squares = tile_set.reshape(tile_count, tile_size, tile_size)
    positions = places.reshape(tile_count)
    tile_row = positions // per_row
    tile_col = positions % per_row
    pieces = child_vec.reshape(per_row, tile_size, -1)[tile_col]
    product = jnp.einsum("nab,nbw->naw", squares, pieces, precision=highest)
    chooser = (
        jnp.arange(col_size // tile_size, dtype=jnp.int32)[:, None] == tile_row[None, :]
    ).astype(jnp.float32)
    return jnp.einsum("kn,naw->kaw", chooser, product, precision=highest).reshape(col_size, -1)


def lower_tiles(tile_set, places, parent_cols, own_count):
    tile_count = places.shape[-1]
    tile_size = tile_set.shape[-1]
    per_row = own_count // tile_size
    squares = tile_set.reshape(tile_count, tile_size, tile_size)
    positions = places.reshape(tile_count)
    tile_row = positions // per_row
    tile_col = positions % per_row
    pieces = parent_cols.reshape(parent_cols.shape[0] // tile_size, tile_size, -1)[tile_row]
    product = jnp.einsum("nba,nbw->naw", squares, pieces, precision=highest)
    chooser = (jnp.arange(per_row, dtype=jnp.int32)[:, None] == tile_col[None, :]).astype(
        jnp.float32
    )
    return jnp.einsum("kn,naw->kaw", chooser, product, precision=highest).reshape(own_count, -1)


def body(
    rhs_top,
    rhs_mid,
    rhs_low,
    inverse_top,
    inverse_mid,
    inverse_low,
    tiles_mid,
    places_mid,
    tiles_low,
    places_low,
):
    own_count = rhs_top.shape[0]
    leaf_count = lax.axis_size("leaf")
    leaf_bits = leaf_count.bit_length() - 1
    row_count = lax.axis_size("row")
    leaf_index = lax.axis_index("leaf")
    row_index = lax.axis_index("row")
    col_index = lax.axis_index("col")

    def placing(depth_level, col_size):
        leaf_span = leaf_count >> depth_level
        v_offset = (leaf_index % leaf_span * row_count + row_index) * own_count
        return v_offset - col_index * col_size

    size_top = inverse_top.shape[1]
    size_mid = inverse_mid.shape[1]
    size_low = inverse_low.shape[1]
    shift_top = placing(0, size_top)
    shift_mid = placing(1, size_mid)
    shift_low = placing(2, size_low)
    bits_mid = leaf_bits - 1
    bits_low = leaf_bits - 2
    base_low = group_total(into_columns(rhs_low, shift_low, size_low), bits_low)
    base_mid = group_total(into_columns(rhs_mid, shift_mid, size_mid), bits_mid)
    base_top = group_total(into_columns(rhs_top, shift_top, size_top), leaf_bits)
    low_y = col_total(forward(inverse_low, base_low))
    mid_cols = base_mid - group_total(lift_tiles(tiles_low, places_low, low_y, size_mid), bits_mid)
    mid_y = col_total(forward(inverse_mid, mid_cols))
    top_cols = base_top - group_total(lift_tiles(tiles_mid, places_mid, mid_y, size_top), leaf_bits)
    top_y = col_total(forward(inverse_top, top_cols))
    back_top = group_total(backward(inverse_top, top_y), leaf_bits)
    solved_top, down_mid = col_pair(
        from_columns(back_top, shift_top, own_count),
        lower_tiles(tiles_mid, places_mid, back_top, own_count),
    )
    back_mid = group_total(backward(inverse_mid, mid_y - down_mid), bits_mid)
    solved_mid, down_low = col_pair(
        from_columns(back_mid, shift_mid, own_count),
        lower_tiles(tiles_low, places_low, back_mid, own_count),
    )
    back_low = group_total(backward(inverse_low, low_y - down_low), bits_low)
    solved_low = col_total(from_columns(back_low, shift_low, own_count))
    return (solved_top, solved_mid, solved_low)


def solution(mesh):
    return jax.shard_map(
        body,
        mesh=mesh,
        in_specs=(
            P(("leaf", "row"), None),
            P(("leaf", "row"), None),
            P(("leaf", "row"), None),
            P(("leaf", "row"), "col"),
            P(("leaf", "row"), "col"),
            P(("leaf", "row"), "col"),
            P("leaf", "row", "col", None, None, None),
            P("leaf", "row", "col", None),
            P("leaf", "row", "col", None, None, None),
            P("leaf", "row", "col", None),
        ),
        out_specs=(P(("leaf", "row"), None), P(("leaf", "row"), None), P(("leaf", "row"), None)),
        check_vma=False,
    )
```

profile of v0, /device:TPU:1, one launch (start us, length us, event | category | flops | bytes accessed | tf_op | source)
XLA Modules:
  0.0 885.7 jit_solution(1058798755863715967)
XLA Ops:
  7.2 0.8 copy.17
  8.7 0.7 reshape.142
  10.4 0.8 reshape.141
  11.3 60.5 %reduce-scatter.13.cloned.1.call-done = f32[16,128]{1,0:T(8,128)} async-done(((f32[256,128]{1,0:T(8,128)}), f32[16,128]{1,0:T(8,128)}) %reduce-scatter.13.cloned.1.call-update) | async-done | bytes 8208 | tf_op jit(solution)/shard_map/reduce_scatter | solution.py:22
  71.8 24.7 %all_gather.26 = f32[256,128]{1,0:T(8,128)S(1)} all-gather(f32[16,128]{1,0:T(8,128)} %reduce-scatter.13.cloned.1.call-done), channel_id=1, replica_groups=mesh['leaf'=4,'row'=16,'col'=4] {'row'}, dimensions={0}, use_global_device_ids=true | all-gather | bytes 139264 | tf_op jit(solution)/shard_map/all_gather | solution.py:25
  97.2 32.0 %psum.56 = f32[128,64]{0,1:T(8,128)S(1)} all-reduce(f32[128,64]{0,1:T(8,128)S(1)} %convolution_bitcast_fusion.7), channel_id=1, replica_groups=mesh['leaf'=4,'row'=16,'col'=4] {'col'}, use_global_device_ids=true, to_apply=%region_3.4 | all-reduce | flops 8192 | bytes 65536 | tf_op jit(solution)/shard_map/psum | solution.py:30
  130.4 0.8 reshape_reshape.12
  132.2 1.0 reshape.140
  133.3 10.0 %reduce-scatter.11.cloned.1.call-done = f32[32,128]{1,0:T(8,128)} async-done(((f32[512,128]{1,0:T(8,128)}), f32[32,128]{1,0:T(8,128)}) %reduce-scatter.11.cloned.1.call-update) | async-done | bytes 16400 | tf_op jit(solution)/shard_map/reduce_scatter | solution.py:22
  143.2 1.2 collective-permute-start.2
  144.5 2.0 collective-permute-done.2
  146.4 0.7 add.158
  147.2 66.3 %reduce-scatter.15.cloned.1.call-done = f32[32,128]{1,0:T(8,128)} async-done(((f32[512,128]{1,0:T(8,128)}), f32[32,128]{1,0:T(8,128)}) %reduce-scatter.15.cloned.1.call-update) | async-done | bytes 16400 | tf_op jit(solution)/shard_map/reduce_scatter | solution.py:22
  213.5 1.0 collective-permute-start.3
  214.5 25.0 %all_gather.25 = f32[512,128]{1,0:T(8,128)S(1)} all-gather(f32[32,128]{1,0:T(8,128)S(1)} %add.158), channel_id=1, replica_groups=mesh['leaf'=4,'row'=16,'col'=4] {'row'}, dimensions={0}, use_global_device_ids=true | all-gather | bytes 278528 | tf_op jit(solution)/shard_map/all_gather | solution.py:25
  239.5 0.7 add.160
  240.2 26.5 %all_gather.27 = f32[512,128]{1,0:T(8,128)S(1)} all-gather(f32[32,128]{1,0:T(8,128)S(1)} %add.160), channel_id=1, replica_groups=mesh['leaf'=4,'row'=16,'col'=4] {'row'}, dimensions={0}, use_global_device_ids=true | all-gather | bytes 278528 | tf_op jit(solution)/shard_map/all_gather | solution.py:25
  267.0 1.0 convolution_bitcast_fusion.6
  268.0 37.9 %psum.57 = f32[128,64]{0,1:T(8,128)S(1)} all-reduce(f32[128,64]{0,1:T(8,128)S(1)} %convolution_bitcast_fusion.6), channel_id=1, replica_groups=mesh['leaf'=4,'row'=16,'col'=4] {'col'}, use_global_device_ids=true, to_apply=%region_5.6 | all-reduce | flops 8192 | bytes 65536 | tf_op jit(solution)/shard_map/psum | solution.py:30
  306.0 0.6 fusion.1
  307.5 1.0 reshape_reshape.13
  308.6 1.1 collective-permute-start
  309.8 1.9 collective-permute-done
  311.7 0.8 add.153
  312.4 2.8 collective-permute-start.1
  315.3 52.2 %reduce-scatter.17.cloned.1.call-done = f32[64,128]{1,0:T(8,128)} async-done(((f32[1024,128]{1,0:T(8,128)}), f32[64,128]{1,0:T(8,128)}) %reduce-scatter.17.cloned.1.call-update) | async-done | bytes 32784 | tf_op jit(solution)/shard_map/reduce_scatter | solution.py:22
  367.4 1.2 collective-permute-start.4
  368.7 2.2 collective-permute-done.4
  370.8 0.8 add.161
  371.6 2.7 collective-permute-start.5
  374.3 26.6 %all_gather.24 = f32[1024,128]{1,0:T(8,128)S(1)} all-gather(f32[64,128]{1,0:T(8,128)S(1)} %add.154), channel_id=1, replica_groups=mesh['leaf'=4,'row'=16,'col'=4] {'row'}, dimensions={0}, use_global_device_ids=true | all-gather | bytes 557056 | tf_op jit(solution)/shard_map/all_gather | solution.py:25
  400.9 27.0 %all_gather.28 = f32[1024,128]{1,0:T(8,128)S(1)} all-gather(f32[64,128]{1,0:T(8,128)S(1)} %add.162), channel_id=1, replica_groups=mesh['leaf'=4,'row'=16,'col'=4] {'row'}, dimensions={0}, use_global_device_ids=true | all-gather | bytes 557056 | tf_op jit(solution)/shard_map/all_gather | solution.py:25
  428.1 1.8 convolution_bitcast_fusion.5
  430.0 40.2 %psum.58 = f32[128,64]{0,1:T(8,128)S(1)} all-reduce(f32[128,64]{0,1:T(8,128)S(1)} %convolution_bitcast_fusion.5), channel_id=1, replica_groups=mesh['leaf'=4,'row'=16,'col'=4] {'col'}, use_global_device_ids=true, to_apply=%region_7.8 | all-reduce | flops 8192 | bytes 65536 | tf_op jit(solution)/shard_map/psum | solution.py:30
  470.2 0.7 convolution_bitcast_fusion
  471.2 1.0 reshape.148
  472.3 56.4 %reduce-scatter.19.cloned.1.call-done = f32[64,128]{1,0:T(8,128)} async-done(((f32[1024,128]{1,0:T(8,128)}), f32[64,128]{1,0:T(8,128)}) %reduce-scatter.19.cloned.1.call-update) | async-done | bytes 32784 | tf_op jit(solution)/shard_map/reduce_scatter | solution.py:22
  528.7 1.2 collective-permute-start.6
  529.9 2.2 collective-permute-done.6
  532.1 0.8 add.163
  532.8 2.7 collective-permute-start.7
  535.6 1.5 collective-permute-done.7
  537.1 26.5 %all_gather.29 = f32[1024,128]{1,0:T(8,128)S(1)} all-gather(f32[64,128]{1,0:T(8,128)S(1)} %add.164), channel_id=1, replica_groups=mesh['leaf'=4,'row'=16,'col'=4] {'row'}, dimensions={0}, use_global_device_ids=true | all-gather | bytes 557056 | tf_op jit(solution)/shard_map/all_gather | solution.py:25
  563.8 1.3 gather_fusion
  565.1 1.5 convolution_bitcast_fusion.2
  567.0 33.4 %psum.60 = f32[128,64]{0,1:T(8,128)S(1)} all-reduce(f32[128,64]{0,1:T(8,128)S(1)} %bitcast.66), channel_id=1, replica_groups=mesh['leaf'=4,'row'=16,'col'=4] {'col'}, use_global_device_ids=true, to_apply=%region_10.11 | all-reduce | flops 8192 | bytes 65536 | tf_op jit(solution)/shard_map/psum | solution.py:34
  600.4 1.2 convolution_bitcast_fusion.1
  601.8 0.8 reshape.151
  602.7 58.2 %reduce-scatter.21.cloned.1.call-done = f32[32,128]{1,0:T(8,128)} async-done(((f32[512,128]{1,0:T(8,128)}), f32[32,128]{1,0:T(8,128)}) %reduce-scatter.21.cloned.1.call-update) | async-done | bytes 16400 | tf_op jit(solution)/shard_map/reduce_scatter | solution.py:22
  660.9 1.3 collective-permute-start.8
  662.2 1.9 collective-permute-done.8
  664.1 0.7 add.166
  664.9 25.6 %all_gather.30 = f32[512,128]{1,0:T(8,128)S(1)} all-gather(f32[32,128]{1,0:T(8,128)S(1)} %add.166), channel_id=1, replica_groups=mesh['leaf'=4,'row'=16,'col'=4] {'row'}, dimensions={0}, use_global_device_ids=true | all-gather | bytes 278528 | tf_op jit(solution)/shard_map/all_gather | solution.py:25
  691.8 32.3 %psum.62 = f32[128,64]{0,1:T(8,128)S(1)} all-reduce(f32[128,64]{0,1:T(8,128)S(1)} %bitcast.67), channel_id=1, replica_groups=mesh['leaf'=4,'row'=16,'col'=4] {'col'}, use_global_device_ids=true, to_apply=%region_13.14 | all-reduce | flops 8192 | bytes 65536 | tf_op jit(solution)/shard_map/psum | solution.py:34
  724.5 0.8 reshape.154
  725.5 0.7 pad_dynamic-slice_fusion
  726.3 0.7 pad_dynamic-slice_fusion.1
  727.0 56.7 %reduce-scatter.23.cloned.1.call-done = f32[16,128]{1,0:T(8,128)} async-done(((f32[256,128]{1,0:T(8,128)}), f32[16,128]{1,0:T(8,128)}) %reduce-scatter.23.cloned.1.call-update) | async-done | bytes 8208 | tf_op jit(solution)/shard_map/reduce_scatter | solution.py:22
  783.7 24.6 %all_gather.31 = f32[256,128]{1,0:T(8,128)S(1)} all-gather(f32[16,128]{1,0:T(8,128)} %reduce-scatter.23.cloned.1.call-done), channel_id=1, replica_groups=mesh['leaf'=4,'row'=16,'col'=4] {'row'}, dimensions={0}, use_global_device_ids=true | all-gather | bytes 139264 | tf_op jit(solution)/shard_map/all_gather | solution.py:25
  808.4 0.7 pad_dynamic-slice_fusion.2
  809.0 65.5 %all-reduce.6.cloned.1.call-done = (f32[128,64]{1,0:T(8,128)}, f32[128,64]{1,0:T(8,128)}, f32[128,64]{1,0:T(8,128)}) async-done(((f32[128,64]{1,0:T(8,128)}, f32[128,64]{1,0:T(8,128)}, f32[128,64]{1,0:T(8,128)}), (f32[128,64]{1,0:T(8,128)}, f32[128,64]{1,0:T(8,128)}, f32[128,64]{1,0:T(8,128)})) %all-reduce.6.cloned.1.call-update) | async-done | bytes 98320 | tf_op jit(solution)/shard_map/psum | solution.py:34
  874.5 1.5 copy.25
  876.1 1.5 copy.26
  877.6 1.5 copy.27
  (92 shorter events, 9.3 us)
Async XLA Ops:
  7.2 421.0 %copy-start = (f32[128,2048]{1,0:T(8,128)S(1)}, f32[128,2048]{1,0:T(8,128)}, u32[]{:S(2)}) copy-start(f32[128,2048]{1,0:T(8,128)} %param.13) | copy-start | bytes 3145732
  7.2 2.4 copy-start.9
  7.2 64.7 %reduce-scatter.13.cloned.1.call-start = ((), (), s32[]{:S(2)}) async-start(), calls=%async_computation.10 | async-start | bytes 139264 | tf_op jit(solution)/shard_map/reduce_scatter | solution.py:22
  9.5 133.7 %reduce-scatter.11.cloned.1.call-start = ((), (), s32[]{:S(2)}) async-start(), calls=%async_computation.9 | async-start | bytes 278528 | tf_op jit(solution)/shard_map/reduce_scatter | solution.py:22
  10.3 86.3 %copy-start.3 = (f32[128,512]{1,0:T(8,128)S(1)}, f32[128,512]{1,0:T(8,128)}, u32[]{:S(2)}) copy-start(f32[128,512]{1,0:T(8,128)} %param.15) | copy-start | bytes 786436
  10.4 118.9 %copy-start.5 = (f32[1,1,1,2,128,128]{5,4,3,2,1,0:T(8,128)S(1)}, f32[1,1,1,2,128,128]{5,4,3,2,1,0:T(8,128)}, u32[]{:S(2)}) copy-start(f32[1,1,1,2,128,128]{5,4,3,2,1,0:T(8,128)} %param.18) | copy-start | bytes 393220
  10.4 119.4 %copy-start.11 = (s32[1,1,1,2]{3,2,1,0:T(1,128)S(1)}, s32[1,1,1,2]{3,2,1,0:T(1,128)}, u32[]{:S(2)}) copy-start(s32[1,1,1,2]{3,2,1,0:T(1,128)} %param.19) | copy-start | bytes 28
  11.3 202.2 %reduce-scatter.15.cloned.1.call-start = ((), (), s32[]{:S(2)}) async-start(), calls=%async_computation.11 | async-start | bytes 278528 | tf_op jit(solution)/shard_map/reduce_scatter | solution.py:22
  129.2 0.6 copy-start.6
  129.3 2.0 copy-start.10
  131.3 177.3 %reduce-scatter.9.cloned.1.call-start = ((), (), s32[]{:S(2)}) async-start(), calls=%async_computation.8 | async-start | bytes 557056 | tf_op jit(solution)/shard_map/reduce_scatter | solution.py:22
  133.2 133.7 %copy-start.1 = (f32[128,1024]{1,0:T(8,128)S(1)}, f32[128,1024]{1,0:T(8,128)}, u32[]{:S(2)}) copy-start(f32[128,1024]{1,0:T(8,128)} %param.14) | copy-start | bytes 1572868
  133.2 234.2 %reduce-scatter.17.cloned.1.call-start = ((), (), s32[]{:S(2)}) async-start(), calls=%async_computation.12 | async-start | bytes 557056 | tf_op jit(solution)/shard_map/reduce_scatter | solution.py:22
  143.2 3.2 collective-permute-start.2
  213.5 26.0 %collective-permute-start.3 = (f32[32,128]{1,0:T(8,128)}, f32[32,128]{1,0:T(8,128)S(1)}, u32[]{:S(2)}, u32[]{:S(2)}) collective-permute-start(f32[32,128]{1,0:T(8,128)} %reduce-scatter.15.cloned.1.call-done), channel_id=1, source_target_pairs={{0,64},{64,0},{128,192},{192,128},{1,65},{65,1},{129,193},{193,129... | collective-permute-start | bytes 49160 | tf_op jit(solution)/shard_map/ppermute | solution.py:16
  266.8 39.2 %copy-start.2 = (f32[1,1,1,4,128,128]{5,4,3,2,1,0:T(8,128)S(1)}, f32[1,1,1,4,128,128]{5,4,3,2,1,0:T(8,128)}, u32[]{:S(2)}) copy-start(f32[1,1,1,4,128,128]{5,4,3,2,1,0:T(8,128)} %param.16) | copy-start | bytes 786436
  266.8 39.9 %copy-start.12 = (s32[1,1,1,4]{3,2,1,0:T(1,128)S(1)}, s32[1,1,1,4]{3,2,1,0:T(1,128)}, u32[]{:S(2)}) copy-start(s32[1,1,1,4]{3,2,1,0:T(1,128)} %param.17) | copy-start | bytes 52
  305.9 0.7 copy-start.8
  308.5 220.1 %reduce-scatter.19.cloned.1.call-start = ((), (), s32[]{:S(2)}) async-start(), calls=%async_computation.13 | async-start | bytes 557056 | tf_op jit(solution)/shard_map/reduce_scatter | solution.py:22
  308.6 3.1 collective-permute-start
  312.4 56.2 %collective-permute-start.1 = (f32[64,128]{1,0:T(8,128)S(1)}, f32[64,128]{1,0:T(8,128)S(1)}, u32[]{:S(2)}, u32[]{:S(2)}) collective-permute-start(f32[64,128]{1,0:T(8,128)S(1)} %add.153), channel_id=1, source_target_pairs={{0,128},{128,0},{64,192},{192,64},{1,129},{129,1},{65,193},{193,65... | collective-permute-start | bytes 98312 | tf_op jit(solution)/shard_map/ppermute | solution.py:16
  367.4 3.4 collective-permute-start.4
  371.6 29.3 %collective-permute-start.5 = (f32[64,128]{1,0:T(8,128)S(1)}, f32[64,128]{1,0:T(8,128)S(1)}, u32[]{:S(2)}, u32[]{:S(2)}) collective-permute-start(f32[64,128]{1,0:T(8,128)S(1)} %add.161), channel_id=1, source_target_pairs={{0,128},{128,0},{64,192},{192,64},{1,129},{129,1},{65,193},{193,65... | collective-permute-start | bytes 98312 | tf_op jit(solution)/shard_map/ppermute | solution.py:16
  472.2 188.7 %reduce-scatter.21.cloned.1.call-start = ((), (), s32[]{:S(2)}) async-start(), calls=%async_computation.14 | async-start | bytes 278528 | tf_op jit(solution)/shard_map/reduce_scatter | solution.py:22
  528.7 3.4 collective-permute-start.6
  532.8 4.3 collective-permute-start.7
  602.6 121.5 %copy-start.4 = (f32[128,512]{1,0:T(8,128)S(1)}, f32[128,512]{1,0:T(8,128)}, u32[]{:S(2)}) copy-start(f32[128,512]{1,0:T(8,128)} %param.15) | copy-start | bytes 786436
  602.6 121.5 %copy-start.7 = (f32[128,64]{0,1:T(8,128)S(1)}, f32[128,64]{0,1:T(8,128)}, u32[]{:S(2)}) copy-start(f32[128,64]{0,1:T(8,128)} %copy-done.6) | copy-start | bytes 98308
  602.6 181.1 %reduce-scatter.23.cloned.1.call-start = ((), (), s32[]{:S(2)}) async-start(), calls=%async_computation.15 | async-start | bytes 139264 | tf_op jit(solution)/shard_map/reduce_scatter | solution.py:22
  660.9 3.2 collective-permute-start.8
  725.2 149.3 %all-reduce.6.cloned.1.call-start = ((), (), s32[]{:S(2)}) async-start(), calls=%async_computation.16 | async-start | bytes 393216 | tf_op jit(solution)/shard_map/psum | solution.py:34
Sparse Core Ops, SparseCore 0:
  10.5 61.2 reduce-scatter.12
  74.5 68.7 reduce-scatter.10
  145.7 67.6 reduce-scatter.14
  216.0 69.3 reduce-scatter.8
  308.7 58.7 reduce-scatter.16
  472.3 56.3 reduce-scatter.18
  602.8 58.1 reduce-scatter.20
  725.4 58.2 reduce-scatter.22
  809.2 65.3 all-reduce.5
where the time goes:
time: 887 us; the launch traced here: 886 us
  waiting for transfers between devices  438 us (49%)
  blocking collectives  382 us (43%)
  local copies, waits for them, and re-layouts  21.3 us (2%)
  starting transfers between devices  15.7 us (2%)
  between operations  14.4 us (2%)
  matrix products  9.91 us (1%)
    reduce_scatter x8, waiting for transfers between devices, group_total(): lax.psum_scatter(folded, 'row', scatter_dimension=0, tiled=True)  360 us
    all_gather x8, blocking collectives, group_total(): summed = lax.all_gather(share_part, 'row', axis=0, tiled=True)  206 us
    psum x3, blocking collectives, col_total(): return lax.psum(part, 'col')  110 us
    psum x2, blocking collectives, col_pair(): return lax.psum((first_part, second_part), 'col')  65.7 us
    psum x1, waiting for transfers between devices, col_pair(): return lax.psum((first_part, second_part), 'col')  65.5 us
  transfers between devices with their start and end apart: 18, of which 14 were waited for; matrix products, arithmetic and copies ran while one was open for 2% of the time, Pallas kernels for 0%

commit v1 on v0

--- a/solution.py
+++ b/solution.py
@@ -22,7 +22,9 @@
     share_part = lax.psum_scatter(folded, "row", scatter_dimension=0, tiled=True)
     for bit_index in range(leaf_bits_used):
         share_part = share_part + partner(share_part, "leaf", bit_index)
-    summed = lax.all_gather(share_part, "row", axis=0, tiled=True)
+    summed = jnp.concatenate(
+        lax.all_to_all(jnp.stack([share_part] * lax.axis_size("row")), "row", 0, 0), axis=0
+    )
     return summed.reshape(col_size, vec_width)
 
 

time: 887 us -> 794 us (0.90)
  blocking collectives: 382 us -> 154 us
  waiting for transfers between devices: 438 us -> 532 us
  starting transfers between devices: 15.7 us -> 49 us
    all_gather x8 -> x0, blocking collectives: 206 us -> none  [group_total(): summed = lax.all_gather(share_part, 'row', axis=0, tiled=True)]
    reduce_scatter x8, waiting for transfers between devices: 360 us -> 417 us  [group_total(): lax.psum_scatter(folded, 'row', scatter_dimension=0, tiled=True)]
    all_to_all x0 -> x7, waiting for transfers between devices: none -> 42.3 us  [group_total(): lax.all_to_all(jnp.stack([share_part] * lax.axis_size('row')), 'row', 0, 0)]
    all_to_all x0 -> x7, starting transfers between devices: none -> 32.3 us  [group_total(): lax.all_to_all(jnp.stack([share_part] * lax.axis_size('row')), 'row', 0, 0)]
    psum x3, blocking collectives: 110 us -> 81.8 us  [col_total(): return lax.psum(part, 'col')]
    all_to_all x0 -> x1, blocking collectives: none -> 17 us  [group_total(): lax.all_to_all(jnp.stack([share_part] * lax.axis_size('row')), 'row', 0, 0)]
    psum x2, blocking collectives: 65.7 us -> 55.4 us  [col_pair(): return lax.psum((first_part, second_part), 'col')]
    psum x1, waiting for transfers between devices: 65.5 us -> 55.7 us  [col_pair(): return lax.psum((first_part, second_part), 'col')]
  transfers between devices with their start and end apart: 18 -> 25, of which waited for: 14 -> 23; matrix products, arithmetic and copies ran while one was open for 2% -> 2% of each run, Pallas kernels for 0% -> 0%
where the time goes in v1:
time: 794 us; the launch traced here: 792 us
  waiting for transfers between devices  532 us (67%)
  blocking collectives  154 us (19%)
  starting transfers between devices  49 us (6%)
  local copies, waits for them, and re-layouts  27.9 us (4%)
  between operations  14.5 us (2%)
  matrix products  9.15 us (1%)
    reduce_scatter x8, waiting for transfers between devices, group_total(): lax.psum_scatter(folded, 'row', scatter_dimension=0, tiled=True)  417 us
    psum x3, blocking collectives, col_total(): return lax.psum(part, 'col')  81.8 us
    psum x1, waiting for transfers between devices, col_pair(): return lax.psum((first_part, second_part), 'col')  55.7 us
    psum x2, blocking collectives, col_pair(): return lax.psum((first_part, second_part), 'col')  55.4 us
    all_to_all x7, waiting for transfers between devices, group_total(): lax.all_to_all(jnp.stack([share_part] * lax.axis_size('row')), 'row', 0, 0)  42.3 us
    all_to_all x7, starting transfers between devices, group_total(): lax.all_to_all(jnp.stack([share_part] * lax.axis_size('row')), 'row', 0, 0)  32.3 us
    ppermute x9, waiting for transfers between devices, partner(): return lax.ppermute(block, axis, route)  17.5 us
    all_to_all x1, blocking collectives, group_total(): lax.all_to_all(jnp.stack([share_part] * lax.axis_size('row')), 'row', 0, 0)  17 us
  transfers between devices with their start and end apart: 25, of which 23 were waited for; matrix products, arithmetic and copies ran while one was open for 2% of the time, Pallas kernels for 0%

profile of v1, /device:TPU:1, one launch (start us, length us, event | category | flops | bytes accessed | tf_op | source)
XLA Modules:
  0.0 792.3 jit_solution(14303943591055082367)
XLA Ops:
  7.2 0.8 copy.17
  9.5 62.3 %reduce-scatter.13.cloned.1.call-done = f32[16,128]{1,0:T(8,128)} async-done(((f32[256,128]{1,0:T(8,128)}), f32[16,128]{1,0:T(8,128)}) %reduce-scatter.13.cloned.1.call-update) | async-done | bytes 8208 | tf_op jit(solution)/shard_map/reduce_scatter | solution.py:22
  71.8 1.3 stack.18
  73.2 4.7 all-to-all-start.2
  78.8 0.8 reshape.141
  79.7 6.6 all-to-all-done.2
  87.0 27.2 %psum.56 = f32[128,64]{0,1:T(8,128)S(1)} all-reduce(f32[128,64]{0,1:T(8,128)S(1)} %convolution_bitcast_fusion.7), channel_id=1, replica_groups=mesh['leaf'=4,'row'=16,'col'=4] {'col'}, use_global_device_ids=true, to_apply=%region_3.4 | all-reduce | flops 8192 | bytes 65536 | tf_op jit(solution)/shard_map/psum | solution.py:32
  115.4 0.8 reshape_reshape.23
  116.3 36.4 %reduce-scatter.11.cloned.1.call-done = f32[32,128]{1,0:T(8,128)} async-done(((f32[512,128]{1,0:T(8,128)}), f32[32,128]{1,0:T(8,128)}) %reduce-scatter.11.cloned.1.call-update) | async-done | bytes 16400 | tf_op jit(solution)/shard_map/reduce_scatter | solution.py:22
  152.7 1.2 collective-permute-start.2
  153.9 2.0 collective-permute-done.2
  157.4 5.1 all-to-all-start.1
  162.5 61.4 %reduce-scatter.15.cloned.1.call-done = f32[32,128]{1,0:T(8,128)} async-done(((f32[512,128]{1,0:T(8,128)}), f32[32,128]{1,0:T(8,128)}) %reduce-scatter.15.cloned.1.call-update) | async-done | bytes 16400 | tf_op jit(solution)/shard_map/reduce_scatter | solution.py:22
  223.8 1.2 collective-permute-start.3
  225.1 2.0 collective-permute-done.3
  228.5 4.2 all-to-all-start.3
  233.6 1.0 reshape.140
  234.7 7.6 all-to-all-done.3
  242.3 1.0 sub.36
  243.5 1.0 convolution_bitcast_fusion.6
  244.5 27.4 %psum.57 = f32[128,64]{0,1:T(8,128)S(1)} all-reduce(f32[128,64]{0,1:T(8,128)S(1)} %convolution_bitcast_fusion.6), channel_id=1, replica_groups=mesh['leaf'=4,'row'=16,'col'=4] {'col'}, use_global_device_ids=true, to_apply=%region_5.6 | all-reduce | flops 8192 | bytes 65536 | tf_op jit(solution)/shard_map/psum | solution.py:32
  273.5 1.0 reshape_reshape.24
  274.5 33.5 %reduce-scatter.9.cloned.1.call-done = f32[64,128]{1,0:T(8,128)} async-done(((f32[1024,128]{1,0:T(8,128)}), f32[64,128]{1,0:T(8,128)}) %reduce-scatter.9.cloned.1.call-update) | async-done | bytes 32784 | tf_op jit(solution)/shard_map/reduce_scatter | solution.py:22
  308.0 2.4 collective-permute-start
  310.4 1.9 collective-permute-done
  313.0 1.9 collective-permute-start.1
  314.9 2.4 collective-permute-done.1
  317.3 0.9 stack.16
  318.2 4.2 all-to-all-start
  322.4 57.9 %reduce-scatter.17.cloned.1.call-done = f32[64,128]{1,0:T(8,128)} async-done(((f32[1024,128]{1,0:T(8,128)}), f32[64,128]{1,0:T(8,128)}) %reduce-scatter.17.cloned.1.call-update) | async-done | bytes 32784 | tf_op jit(solution)/shard_map/reduce_scatter | solution.py:22
  380.3 1.8 collective-permute-start.4
  382.1 1.9 collective-permute-done.4
  384.7 2.4 collective-permute-start.5
  387.1 1.9 collective-permute-done.5
  389.1 17.0 %all_to_all.40 = f32[16,64,128]{2,1,0:T(8,128)S(1)} all-to-all(f32[16,64,128]{2,1,0:T(8,128)S(1)} %stack.20), channel_id=1, replica_groups=mesh['leaf'=4,'row'=16,'col'=4] {'row'}, dimensions={0} | all-to-all | bytes 1048576 | tf_op jit(solution)/shard_map/all_to_all | solution.py:26
  406.3 1.8 convolution_bitcast_fusion.5
  408.2 27.2 %psum.58 = f32[128,64]{0,1:T(8,128)S(1)} all-reduce(f32[128,64]{0,1:T(8,128)S(1)} %convolution_bitcast_fusion.5), channel_id=1, replica_groups=mesh['leaf'=4,'row'=16,'col'=4] {'col'}, use_global_device_ids=true, to_apply=%region_7.8 | all-reduce | flops 8192 | bytes 65536 | tf_op jit(solution)/shard_map/psum | solution.py:32
  436.4 1.0 reshape.147
  437.5 56.2 %reduce-scatter.19.cloned.1.call-done = f32[64,128]{1,0:T(8,128)} async-done(((f32[1024,128]{1,0:T(8,128)}), f32[64,128]{1,0:T(8,128)}) %reduce-scatter.19.cloned.1.call-update) | async-done | bytes 32784 | tf_op jit(solution)/shard_map/reduce_scatter | solution.py:22
  493.6 1.2 collective-permute-start.6
  494.8 2.2 collective-permute-done.6
  497.8 2.7 collective-permute-start.7
  500.5 1.5 collective-permute-done.7
  502.0 0.9 stack.21
  502.9 4.4 all-to-all-start.5
  507.4 11.8 %all-to-all-done.5 = f32[16,64,128]{2,1,0:T(8,128)S(1)} async-done(((f32[16,64,128]{2,1,0:T(8,128)}), f32[16,64,128]{2,1,0:T(8,128)S(1)}, u32[]{:S(2)}, u32[]{:S(2)}) %all-to-all-start.5) | async-done | bytes 524320 | tf_op jit(solution)/shard_map/all_to_all | solution.py:26
  519.4 1.3 gather_fusion
  520.7 1.5 convolution_bitcast_fusion.2
  522.5 28.2 %psum.60 = f32[128,64]{0,1:T(8,128)S(1)} all-reduce(f32[128,64]{0,1:T(8,128)S(1)} %bitcast.66), channel_id=1, replica_groups=mesh['leaf'=4,'row'=16,'col'=4] {'col'}, use_global_device_ids=true, to_apply=%region_10.11 | all-reduce | flops 8192 | bytes 65536 | tf_op jit(solution)/shard_map/psum | solution.py:36
  551.4 0.8 reshape.149
  552.2 54.7 %reduce-scatter.21.cloned.1.call-done = f32[32,128]{1,0:T(8,128)} async-done(((f32[512,128]{1,0:T(8,128)}), f32[32,128]{1,0:T(8,128)}) %reduce-scatter.21.cloned.1.call-update) | async-done | bytes 16400 | tf_op jit(solution)/shard_map/reduce_scatter | solution.py:22
  607.0 1.4 collective-permute-start.8
  608.3 1.8 collective-permute-done.8
  611.6 5.0 all-to-all-start.6
  616.7 9.5 %all-to-all-done.6 = f32[16,32,128]{2,1,0:T(8,128)S(1)} async-done(((f32[16,32,128]{2,1,0:T(8,128)}), f32[16,32,128]{2,1,0:T(8,128)S(1)}, u32[]{:S(2)}, u32[]{:S(2)}) %all-to-all-start.6) | async-done | bytes 262176 | tf_op jit(solution)/shard_map/all_to_all | solution.py:26
  627.6 27.2 %psum.62 = f32[128,64]{0,1:T(8,128)S(1)} all-reduce(f32[128,64]{0,1:T(8,128)S(1)} %bitcast.67), channel_id=1, replica_groups=mesh['leaf'=4,'row'=16,'col'=4] {'col'}, use_global_device_ids=true, to_apply=%region_13.14 | all-reduce | flops 8192 | bytes 65536 | tf_op jit(solution)/shard_map/psum | solution.py:36
  656.0 54.2 %reduce-scatter.23.cloned.1.call-done = f32[16,128]{1,0:T(8,128)} async-done(((f32[256,128]{1,0:T(8,128)}), f32[16,128]{1,0:T(8,128)}) %reduce-scatter.23.cloned.1.call-update) | async-done | bytes 8208 | tf_op jit(solution)/shard_map/reduce_scatter | solution.py:22
  710.2 1.4 stack.23
  711.5 4.7 all-to-all-start.7
  718.0 6.7 all-to-all-done.7
  725.5 55.7 %all-reduce.6.cloned.1.call-done = (f32[128,64]{1,0:T(8,128)}, f32[128,64]{1,0:T(8,128)}, f32[128,64]{1,0:T(8,128)}) async-done(((f32[128,64]{1,0:T(8,128)}, f32[128,64]{1,0:T(8,128)}, f32[128,64]{1,0:T(8,128)}), (f32[128,64]{1,0:T(8,128)}, f32[128,64]{1,0:T(8,128)}, f32[128,64]{1,0:T(8,128)})) %all-reduce.6.cloned.1.call-update) | async-done | bytes 98320 | tf_op jit(solution)/shard_map/psum | solution.py:36
  781.2 1.5 copy.25
  782.7 1.5 copy.26
  784.3 1.5 copy.27
  (107 shorter events, 21.1 us)
Async XLA Ops:
  7.2 399.2 %copy-start = (f32[128,2048]{1,0:T(8,128)S(1)}, f32[128,2048]{1,0:T(8,128)}, u32[]{:S(2)}) copy-start(f32[128,2048]{1,0:T(8,128)} %param.13) | copy-start | bytes 3145732
  7.2 70.7 %copy-start.9 = (f32[128,64]{0,1:T(8,128)S(1)}, f32[128,64]{0,1:T(8,128)}, u32[]{:S(2)}) copy-start(f32[128,64]{0,1:T(8,128)} %param.11) | copy-start | bytes 98308
  7.2 64.7 %reduce-scatter.13.cloned.1.call-start = ((), (), s32[]{:S(2)}) async-start(), calls=%async_computation.18 | async-start | bytes 139264 | tf_op jit(solution)/shard_map/reduce_scatter | solution.py:22
  73.2 13.1 %all-to-all-start.2 = ((f32[16,16,128]{2,1,0:T(8,128)}), f32[16,16,128]{2,1,0:T(8,128)S(1)}, u32[]{:S(2)}, u32[]{:S(2)}) async-start(f32[16,16,128]{2,1,0:T(8,128)} %stack.18), calls=%async_computation.5 | async-start | bytes 262144 | tf_op jit(solution)/shard_map/all_to_all | solution.py:26
  77.9 74.8 %reduce-scatter.11.cloned.1.call-start = ((), (), s32[]{:S(2)}) async-start(), calls=%async_computation.17 | async-start | bytes 278528 | tf_op jit(solution)/shard_map/reduce_scatter | solution.py:22
  78.7 7.7 copy-start.3
  78.7 35.6 %copy-start.5 = (f32[1,1,1,2,128,128]{5,4,3,2,1,0:T(8,128)S(1)}, f32[1,1,1,2,128,128]{5,4,3,2,1,0:T(8,128)}, u32[]{:S(2)}) copy-start(f32[1,1,1,2,128,128]{5,4,3,2,1,0:T(8,128)} %param.18) | copy-start | bytes 393220
  78.7 36.1 %copy-start.11 = (s32[1,1,1,2]{3,2,1,0:T(1,128)S(1)}, s32[1,1,1,2]{3,2,1,0:T(1,128)}, u32[]{:S(2)}) copy-start(s32[1,1,1,2]{3,2,1,0:T(1,128)} %param.19) | copy-start | bytes 28
  79.6 144.2 %reduce-scatter.15.cloned.1.call-start = ((), (), s32[]{:S(2)}) async-start(), calls=%async_computation.19 | async-start | bytes 278528 | tf_op jit(solution)/shard_map/reduce_scatter | solution.py:22
  114.2 0.6 copy-start.7
  116.2 116.5 %copy-start.10 = (f32[128,64]{0,1:T(8,128)S(1)}, f32[128,64]{0,1:T(8,128)}, u32[]{:S(2)}) copy-start(f32[128,64]{0,1:T(8,128)} %param.10) | copy-start | bytes 98308
  152.7 3.2 collective-permute-start.2
  157.4 70.4 %all-to-all-start.1 = ((f32[16,32,128]{2,1,0:T(8,128)}), f32[16,32,128]{2,1,0:T(8,128)S(1)}, u32[]{:S(2)}, u32[]{:S(2)}) async-start(f32[16,32,128]{2,1,0:T(8,128)} %stack.17), calls=%async_computation.3 | async-start | bytes 524288 | tf_op jit(solution)/shard_map/all_to_all | solution.py:26
  223.8 3.2 collective-permute-start.3
  228.5 13.8 %all-to-all-start.3 = ((f32[16,32,128]{2,1,0:T(8,128)}), f32[16,32,128]{2,1,0:T(8,128)}, u32[]{:S(2)}, u32[]{:S(2)}) async-start(f32[16,32,128]{2,1,0:T(8,128)} %stack.19), calls=%async_computation.7 | async-start | bytes 524288 | tf_op jit(solution)/shard_map/all_to_all | solution.py:26
  232.7 75.3 %reduce-scatter.9.cloned.1.call-start = ((), (), s32[]{:S(2)}) async-start(), calls=%async_computation.16 | async-start | bytes 557056 | tf_op jit(solution)/shard_map/reduce_scatter | solution.py:22
  234.6 8.8 %copy-start.1 = (f32[128,1024]{1,0:T(8,128)S(1)}, f32[128,1024]{1,0:T(8,128)}, u32[]{:S(2)}) copy-start(f32[128,1024]{1,0:T(8,128)} %param.14) | copy-start | bytes 1572868
  234.6 145.6 %reduce-scatter.17.cloned.1.call-start = ((), (), s32[]{:S(2)}) async-start(), calls=%async_computation.20 | async-start | bytes 557056 | tf_op jit(solution)/shard_map/reduce_scatter | solution.py:22
  243.3 28.7 %copy-start.2 = (f32[1,1,1,4,128,128]{5,4,3,2,1,0:T(8,128)S(1)}, f32[1,1,1,4,128,128]{5,4,3,2,1,0:T(8,128)}, u32[]{:S(2)}) copy-start(f32[1,1,1,4,128,128]{5,4,3,2,1,0:T(8,128)} %param.16) | copy-start | bytes 786436
  243.3 29.3 %copy-start.12 = (s32[1,1,1,4]{3,2,1,0:T(1,128)S(1)}, s32[1,1,1,4]{3,2,1,0:T(1,128)}, u32[]{:S(2)}) copy-start(s32[1,1,1,4]{3,2,1,0:T(1,128)} %param.17) | copy-start | bytes 52
  308.0 4.3 collective-permute-start
  313.0 4.3 collective-permute-start.1
  318.2 70.9 %all-to-all-start = ((f32[16,64,128]{2,1,0:T(8,128)}), f32[16,64,128]{2,1,0:T(8,128)S(1)}, u32[]{:S(2)}, u32[]{:S(2)}) async-start(f32[16,64,128]{2,1,0:T(8,128)} %stack.16), calls=%async_computation.1 | async-start | bytes 1048576 | tf_op jit(solution)/shard_map/all_to_all | solution.py:26
  322.3 171.3 %reduce-scatter.19.cloned.1.call-start = ((), (), s32[]{:S(2)}) async-start(), calls=%async_computation.21 | async-start | bytes 557056 | tf_op jit(solution)/shard_map/reduce_scatter | solution.py:22
  380.3 3.7 collective-permute-start.4
  384.7 4.3 collective-permute-start.5
  493.6 3.4 collective-permute-start.6
  497.8 4.3 collective-permute-start.7
  502.9 16.3 %all-to-all-start.5 = ((f32[16,64,128]{2,1,0:T(8,128)}), f32[16,64,128]{2,1,0:T(8,128)S(1)}, u32[]{:S(2)}, u32[]{:S(2)}) async-start(f32[16,64,128]{2,1,0:T(8,128)} %stack.21), calls=%async_computation.11 | async-start | bytes 1048576 | tf_op jit(solution)/shard_map/all_to_all | solution.py:26
  507.3 99.6 %reduce-scatter.21.cloned.1.call-start = ((), (), s32[]{:S(2)}) async-start(), calls=%async_computation.22 | async-start | bytes 278528 | tf_op jit(solution)/shard_map/reduce_scatter | solution.py:22
  552.2 74.8 %copy-start.6 = (f32[1,1,1,2,128,128]{5,4,3,2,1,0:T(8,128)S(1)}, f32[1,1,1,2,128,128]{5,4,3,2,1,0:T(8,128)}, u32[]{:S(2)}) copy-start(f32[1,1,1,2,128,128]{5,4,3,2,1,0:T(8,128)} %param.18) | copy-start | bytes 393220
  607.0 3.2 collective-permute-start.8
  610.9 43.9 %copy-start.4 = (f32[128,512]{1,0:T(8,128)S(1)}, f32[128,512]{1,0:T(8,128)}, u32[]{:S(2)}) copy-start(f32[128,512]{1,0:T(8,128)} %param.15) | copy-start | bytes 786436
  610.9 43.9 %copy-start.8 = (f32[128,64]{0,1:T(8,128)S(1)}, f32[128,64]{0,1:T(8,128)}, u32[]{:S(2)}) copy-start(f32[128,64]{0,1:T(8,128)} %copy-done.7) | copy-start | bytes 98308
  611.6 14.7 %all-to-all-start.6 = ((f32[16,32,128]{2,1,0:T(8,128)}), f32[16,32,128]{2,1,0:T(8,128)S(1)}, u32[]{:S(2)}, u32[]{:S(2)}) async-start(f32[16,32,128]{2,1,0:T(8,128)} %stack.22), calls=%async_computation.13 | async-start | bytes 524288 | tf_op jit(solution)/shard_map/all_to_all | solution.py:26
  616.7 93.5 %reduce-scatter.23.cloned.1.call-start = ((), (), s32[]{:S(2)}) async-start(), calls=%async_computation.23 | async-start | bytes 139264 | tf_op jit(solution)/shard_map/reduce_scatter | solution.py:22
  711.5 13.2 %all-to-all-start.7 = ((f32[16,16,128]{2,1,0:T(8,128)}), f32[16,16,128]{2,1,0:T(8,128)S(1)}, u32[]{:S(2)}, u32[]{:S(2)}) async-start(f32[16,16,128]{2,1,0:T(8,128)} %stack.23), calls=%async_computation.15 | async-start | bytes 262144 | tf_op jit(solution)/shard_map/all_to_all | solution.py:26
  716.3 64.9 %all-reduce.6.cloned.1.call-start = ((), (), s32[]{:S(2)}) async-start(), calls=%async_computation.24 | async-start | bytes 393216 | tf_op jit(solution)/shard_map/psum | solution.py:36
Sparse Core Ops, SparseCore 0:
  10.5 61.2 reduce-scatter.12
  81.3 71.3 reduce-scatter.10
  155.2 68.5 reduce-scatter.14
  235.9 72.0 reduce-scatter.8
  310.3 69.9 reduce-scatter.16
  437.6 55.9 reduce-scatter.18
  552.3 54.5 reduce-scatter.20
  656.1 53.9 reduce-scatter.22
  725.6 55.5 all-reduce.5
